TPU v7x, 512 devices: a whole 4x8x8 slice. The times are simulated.
512 devices in a mesh: seq: 128 (over z, y, core), tp: 4 (over x).
Axes of the slice: x: 4, y: 8, z: 8, core: 2. Of those that a mesh axis runs over, the one named last changes fastest.
Arguments:
- hidden_in: bfloat16 [32768, 4096], P('seq', 'tp'), may hold values from -6 to 6
- doc_lengths: int32 [64], replicated, may hold values from 1 to 1024, 32768 in all
- w_query: bfloat16 [4096, 4096], P(None, 'tp'), may hold values from -1 to 1
- w_key: bfloat16 [4096, 1024], P(None, 'tp'), may hold values from -1 to 1
- w_value: bfloat16 [4096, 1024], P(None, 'tp'), may hold values from -0.09375 to 0.09375
- w_out: bfloat16 [4096, 4096], P('tp'), may hold values from -0.09375 to 0.09375
Outputs:
- attn_out: bfloat16 [32768, 4096], P('seq', 'tp')
Inputs may be any that keep to these rules, and one draw needn't show every extreme that they name: `doc_lengths`: every document has 1 to 1024 tokens, the longest exactly 1024, and the lengths sum to 32768.
All inputs are finite; a program needn't handle non-finite values.
Results may differ from a plain program's by a relative error of at most 0.02.
Values may be sent and summed in bfloat16 or wider, within the bound.
A program may use at most 128 MiB of HBM per device.

v0:
```python
import math

import jax
import jax.numpy as jnp
from jax import lax
from jax.sharding import PartitionSpec as P

HEAD_DIM = 128
SPAN = 4


def passed_along(block, axis, distance):
    devices = range(lax.axis_size(axis))
    route = [(i - distance, i) for i in devices if i - distance in devices]
    return lax.ppermute(block, axis, route)


def inverse_frequencies(head_dim):
    exponent = jnp.arange(0, head_dim, 2, dtype=jnp.float32) / head_dim
    base_freq = jnp.power(jnp.float32(500000.0), -exponent)
    wavelength = 2.0 * math.pi / base_freq
    smooth_part = (8192.0 / wavelength - 1.0) / 3.0
    blended = (1.0 - smooth_part) * base_freq / 8.0 + smooth_part * base_freq
    return jnp.where(
        wavelength < 2048.0, base_freq, jnp.where(wavelength > 8192.0, base_freq / 8.0, blended)
    )


def rotary_embed(head_values, positions):
    head_dim = head_values.shape[-1]
    half_dim = head_dim // 2
    frequencies = inverse_frequencies(head_dim)
    angles = positions.astype(jnp.float32)[:, None] * frequencies[None, :]
    cosine = jnp.cos(angles)[:, None, :]
    sine_part = jnp.sin(angles)[:, None, :]
    front_half = head_values[..., :half_dim]
    back_half = head_values[..., half_dim:]
    return jnp.concatenate(
        [front_half * cosine - back_half * sine_part, back_half * cosine + front_half * sine_part],
        axis=-1,
    )


def document_starts(doc_lengths, positions):
    document_ends = jnp.cumsum(doc_lengths)
    picked = jnp.where(document_ends[None, :] <= positions[:, None], doc_lengths[None, :], 0)
    return jnp.sum(picked, axis=1)


def attend_block(running, block, first_key, queries, query_pos, query_start):
    tok_rows = block.shape[1]
    score_scale = 1.0 / math.sqrt(HEAD_DIM)
    key_pos = first_key + jnp.arange(tok_rows, dtype=jnp.int32)

    def update(state):
        peak, total, accum = state
        visible = (key_pos[None, :] >= query_start[:, None]) & (
            key_pos[None, :] <= query_pos[:, None]
        )
        scores = (
            jnp.einsum("qgrd,kgd->grqk", queries, block[0], preferred_element_type=jnp.float32)
            * score_scale
        )
        scores = jnp.where(visible, scores, -1e30)
        new_peak = jnp.maximum(peak, jnp.max(scores, axis=-1))
        weights = jnp.where(visible, jnp.exp(scores - new_peak[..., None]), 0.0)
        factor = jnp.exp(peak - new_peak)
        total = total * factor + jnp.sum(weights, axis=-1)
        accum = accum * factor[..., None] + jnp.einsum(
            "grqk,kgd->grqd",
            weights.astype(jnp.bfloat16),
            block[1],
            preferred_element_type=jnp.float32,
        )
        return (new_peak, total, accum)

    def unchanged(state):
        return state

    needed = (first_key + tok_rows - 1 >= query_start[0]) & (first_key <= query_pos[-1])
    return lax.cond(needed, update, unchanged, running)


def body(hidden_in, doc_lengths, w_query, w_key, w_value, w_out):
    whole = lax.all_gather(hidden_in, "tp", axis=1, tiled=True)
    tok_rows = whole.shape[0]
    shard_index = lax.axis_index("seq")
    query_pos = shard_index * tok_rows + jnp.arange(tok_rows, dtype=jnp.int32)
    query_start = document_starts(doc_lengths, query_pos)
    within = query_pos - query_start
    kv_heads = w_key.shape[1] // HEAD_DIM
    q_heads = w_query.shape[1] // HEAD_DIM
    group = q_heads // kv_heads
    queries = rotary_embed(
        jnp.dot(whole, w_query, preferred_element_type=jnp.float32).reshape(
            tok_rows, q_heads, HEAD_DIM
        ),
        within,
    ).astype(jnp.bfloat16)
    queries = queries.reshape(tok_rows, kv_heads, group, HEAD_DIM)
    keys = rotary_embed(
        jnp.dot(whole, w_key, preferred_element_type=jnp.float32).reshape(
            tok_rows, kv_heads, HEAD_DIM
        ),
        within,
    ).astype(jnp.bfloat16)
    values_local = (
        jnp.dot(whole, w_value, preferred_element_type=jnp.float32)
        .astype(jnp.bfloat16)
        .reshape(tok_rows, kv_heads, HEAD_DIM)
    )
    packed = jnp.stack([keys, values_local])
    initial = (
        jnp.full((kv_heads, group, tok_rows), -1e30, jnp.float32),
        jnp.zeros((kv_heads, group, tok_rows), jnp.float32),
        jnp.zeros((kv_heads, group, tok_rows, HEAD_DIM), jnp.float32),
    )
    running = attend_block(initial, packed, shard_index * tok_rows, queries, query_pos, query_start)
    for distance in range(1, SPAN + 1):
        earlier = passed_along(packed, "seq", distance)
        running = attend_block(
            running, earlier, (shard_index - distance) * tok_rows, queries, query_pos, query_start
        )
    peak, total, accum = running
    context = (
        (accum / total[..., None])
        .transpose(2, 0, 1, 3)
        .reshape(tok_rows, q_heads * HEAD_DIM)
        .astype(jnp.bfloat16)
    )
    partial_value = jnp.dot(context, w_out, preferred_element_type=jnp.float32)
    return lax.psum_scatter(
        partial_value.astype(jnp.bfloat16), "tp", scatter_dimension=1, tiled=True
    )


def solution(mesh):
    return jax.shard_map(
        body,
        mesh=mesh,
        in_specs=(P("seq", "tp"), P(), P(None, "tp"), P(None, "tp"), P(None, "tp"), P("tp", None)),
        out_specs=P("seq", "tp"),
        check_vma=False,
    )
```

profile of v0, /device:TPU:1, one launch (start us, length us, event | category | flops | bytes accessed | tf_op | source)
XLA Modules:
  0.0 164.2 jit_solution(6747039084583784156)
XLA Ops:
  6.5 0.0 copy-start
  6.5 0.0 all-gather.2.cloned.1.call-start
  6.5 0.7 all-gather.2.cloned.1.call-update
  7.3 0.0 reduce-scatter.2.cloned.1.call-start
  7.3 0.6 slice.51
  11.2 0.7 copy.40
  11.9 0.1 reduce-window.8
  12.0 0.1 reduce
  12.1 0.8 select_reduce_fusion
  12.9 0.5 slice.50
  16.7 0.5 multiply_cosine_fusion
  17.3 33.9 %all-gather.2.cloned.1.call-done = bf16[256,4096]{1,0:T(8,128)(2,1)} async-done(((bf16[256,1024]{1,0:T(8,128)(2,1)}), bf16[256,4096]{1,0:T(8,128)(2,1)}) %all-gather.2.cloned.1.call-update) | async-done | bytes 2097168 | tf_op jit(solution)/shard_map/all_gather | solution.py:85
  51.1 0.0 copy-done
  51.1 2.5 %fusion.84 = f32[256,256]{0,1:T(8,128)S(1)} fusion(bf16[256,4096]{1,0:T(8,128)(2,1)} %all-gather.2.cloned.1.call-done, bf16[4096,256]{1,0:T(8,128)(2,1)S(1)} %copy-done), kind=kOutput, calls=%fused_computation.131 | convolution fusion | flops 536870912 | bytes 4456448 | tf_op jit(solution)/shard_map/dot_general | solution.py:102
  53.7 0.1 copy.69
  53.8 0.1 copy.70
  54.0 3.2 %convolution_convert_fusion.1 = bf16[256,256]{0,1:T(8,128)(2,1)S(1)} fusion(bf16[256,4096]{1,0:T(8,128)(2,1)} %all-gather.2.cloned.1.call-done, bf16[4096,256]{1,0:T(8,128)(2,1)} %param.20), kind=kOutput, calls=%fused_computation.112 | convolution fusion | flops 536936448 | bytes 4325376 | tf_op jit(solution)/shard_map/dot_general | solution.py:108
  57.1 0.1 copy.46
  57.2 0.1 subtract_convert_fusion.1
  57.3 0.1 pad_maximum_fusion.1
  57.4 3.7 %collective-permute-start = (bf16[2,256,2,128]{3,1,2,0:T(8,128)(2,1)S(1)}, bf16[2,256,2,128]{3,1,2,0:T(8,128)(2,1)}, u32[]{:S(2)}, u32[]{:S(2)}) collective-permute-start(bf16[2,256,2,128]{3,1,2,0:T(8,128)(2,1)S(1)} %pad_maximum_fusion.1), channel_id=1, source_target_pairs={{0,4},{4,8},{8,12},{12,16},{16,20},{20,24},{24,28},{28,32},{32,36}... | collective-permute-start | bytes 786440 | tf_op jit(solution)/shard_map/ppermute | solution.py:15
  61.1 3.8 %collective-permute-start.1 = (bf16[2,256,2,128]{3,1,2,0:T(8,128)(2,1)S(1)}, bf16[2,256,2,128]{3,1,2,0:T(8,128)(2,1)}, u32[]{:S(2)}, u32[]{:S(2)}) collective-permute-start(bf16[2,256,2,128]{3,1,2,0:T(8,128)(2,1)S(1)} %pad_maximum_fusion.1), channel_id=1, source_target_pairs={{0,8},{4,12},{8,16},{12,20},{16,24},{20,28},{24,32},{28,36},{32,40... | collective-permute-start | bytes 786440 | tf_op jit(solution)/shard_map/ppermute | solution.py:15
  64.9 3.2 %collective-permute-start.2 = (bf16[2,256,2,128]{3,1,2,0:T(8,128)(2,1)S(1)}, bf16[2,256,2,128]{3,1,2,0:T(8,128)(2,1)}, u32[]{:S(2)}, u32[]{:S(2)}) collective-permute-start(bf16[2,256,2,128]{3,1,2,0:T(8,128)(2,1)S(1)} %pad_maximum_fusion.1), channel_id=1, source_target_pairs={{0,12},{4,16},{8,20},{12,24},{16,28},{20,32},{24,36},{28,40},{32,4... | collective-permute-start | bytes 786440 | tf_op jit(solution)/shard_map/ppermute | solution.py:15
  68.1 4.3 %collective-permute-start.3 = (bf16[2,256,2,128]{3,1,2,0:T(8,128)(2,1)S(1)}, bf16[2,256,2,128]{3,1,2,0:T(8,128)(2,1)}, u32[]{:S(2)}, u32[]{:S(2)}) collective-permute-start(bf16[2,256,2,128]{3,1,2,0:T(8,128)(2,1)S(1)} %pad_maximum_fusion.1), channel_id=1, source_target_pairs={{0,16},{4,20},{8,24},{12,28},{16,32},{20,36},{24,40},{28,44},{32,4... | collective-permute-start | bytes 786440 | tf_op jit(solution)/shard_map/ppermute | solution.py:15
  72.4 6.3 %convolution_bitcast_fusion = f32[32,8,8,128]{3,1,2,0:T(8,128)S(1)} fusion(bf16[256,4096]{1,0:T(8,128)(2,1)} %all-gather.2.cloned.1.call-done, bf16[4096,1024]{1,0:T(8,128)(2,1)} %param.18), kind=kOutput, calls=%fused_computation.111 | convolution fusion | flops 2147483648 | bytes 11534336 | tf_op jit(solution)/shard_map/dot_general | solution.py:95
  78.8 0.2 copy.71
  79.0 0.5 subtract_convert_fusion
  79.5 0.1 copy.43
  79.6 0.1 copy.44
  79.7 0.1 pad_maximum_fusion.2
  79.8 0.3 pad_maximum_fusion
  80.1 5.8 %conditional.5 = (f32[2,4,256]{2,1,0:T(4,128)}, f32[2,4,256]{2,1,0:T(4,128)S(1)}, f32[2,4,256,128]{3,2,1,0:T(8,128)}) conditional(s32[]{:T(128)} %convert_element_type.67, () %tuple.38, (s32[256]{0:T(256)S(1)}, s32[256]{0:T(256)S(1)}, bf16[256,2,128]{2,0,1:T(8,128)(2,1)S(1)}, bf16[256,2,4,128]{3,0,2,1:T(8,128)(2,1)S(1)}, ...), branch_computations={%region_2.3_spmd, %region_3.6_spmd} | conditional | flops 275718144 | bytes 8480792 | solution.py:81
  80.1 0.1 compare_and_fusion
  80.2 0.5 fusion
  80.7 0.6 exponential_multiply_fusion
  81.3 1.2 fusion.2
  82.5 0.7 fusion.14
  83.2 2.7 %convolution_add_fusion = f32[2,4,256,128]{3,2,1,0:T(8,128)} fusion(bf16[256,2,128,1]{0,2,3,1:T(8,128)(2,1)S(1)} %bitcast.184, f32[2,256,256,4]{2,1,3,0:T(8,128)S(1)} %get-tuple-element.206, f32[2,4,256]{2,1,0:T(4,128)} %get-tuple-element.234, pred[256,256]{0,1:T(8,128)(4,1)S(1)} %compare_and_fusion, f32[2,4,256]{2,1,0:T(4,128)S(1)} %get-tuple-element.195), kind=kOutput, calls=%fused_computation.5 | convolution fusion | flops 137101312 | bytes 3358720 | tf_op jit(solution)/shard_map/cond/branch_1_fun/grqk,kgd->grqd/dot_general | solution.py:69
  85.9 0.0 collective-permute-done
  85.9 7.3 %conditional.6 = ((f32[2,4,256]{2,1,0:T(4,128)}, f32[2,4,256]{2,1,0:T(4,128)S(1)}, f32[2,4,256,128]{3,2,1,0:T(8,128)})) conditional(s32[]{:T(128)} %convert_element_type.66, (f32[2,4,256]{2,1,0:T(4,128)}, f32[2,4,256]{2,1,0:T(4,128)S(1)}, f32[2,4,256,128]{3,2,1,0:T(8,128)}) %conditional.5, (s32[256]{0:T(256)S(1)}, s32[256]{0:T(256)S(1)}, ...), branch_computations={%region_6.7_spmd, %region_7.10_spmd} | conditional | flops 275976192 | bytes 9571360 | solution.py:81
  85.9 0.1 compare_and_fusion.1
  86.0 1.4 fusion.15
  87.4 0.7 max.8
  88.1 0.5 fusion.17
  88.6 0.7 multiply_add_fusion
  89.4 3.2 %convolution_add_fusion.1 = f32[2,4,256,128]{3,2,1,0:T(8,128)} fusion(f32[2,256,256,4]{2,1,3,0:T(8,128)S(1)} %get-tuple-element.208, f32[2,4,256,128]{3,2,1,0:T(8,128)} %get-tuple-element.122, f32[2,4,256]{2,1,0:T(4,128)S(1)} %max.8, pred[256,256]{0,1:T(8,128)(4,1)S(1)} %compare_and_fusion.1, f32[2,4,256]{2,1,0:T(4,128)S(1)} %bitcast.201, ...), kind=kOutput, calls=%fused_computation.25 | convolution fusion | flops 137363456 | bytes 4407296 | tf_op jit(solution)/shard_map/cond/branch_1_fun/grqk,kgd->grqd/dot_general | solution.py:69
  92.6 0.6 copy.81
  93.2 0.0 collective-permute-done.1
  93.2 0.0 collective-permute-done.2
  93.2 0.0 collective-permute-done.3
  93.3 2.6 %conditional.9 = (f32[2,4,256]{2,1,0:T(4,128)S(1)}, f32[2,4,256,128]{2,3,1,0:T(8,128)}) conditional(s32[]{:T(128)} %convert_element_type.63, (f32[2,4,256]{2,1,0:T(4,128)S(1)}, f32[2,4,256,128]{3,2,1,0:T(8,128)}) %tuple.43, (s32[]{:T(128)}, s32[256]{0:T(256)S(1)}, s32[256]{0:T(256)S(1)}, s32[256]{0:T(256)S(1)}, ...), branch_computations={%region_18.19_spmd, %region_19.22_spmd} | conditional | flops 275976448 | bytes 11654164 | solution.py:81
  93.3 2.5 %copy.67 = f32[2,4,256,128]{2,3,1,0:T(8,128)} copy(f32[2,4,256,128]{3,2,1,0:T(8,128)} %get-tuple-element.193) | data formatting | bytes 2097152 | tf_op jit(solution)/shard_map/cond | solution.py:81
  95.8 1.3 divide_convert_fusion
  97.1 7.1 %convolution_convert_fusion = bf16[256,4096]{1,0:T(8,128)(2,1)} fusion(bf16[256,1024]{0,1:T(8,128)(2,1)S(1)} %bitcast.177, bf16[1024,4096]{1,0:T(8,128)(2,1)} %param.21), kind=kOutput, calls=%fused_computation.110 | convolution fusion | flops 2148532224 | bytes 11010048 | tf_op jit(solution)/shard_map/dot_general | solution.py:131
  104.2 0.0 reduce-scatter.2.cloned.1.call-update
  104.3 53.1 %reduce-scatter.2.cloned.1.call-done = bf16[256,1024]{1,0:T(8,128)(2,1)} async-done(((bf16[256,4096]{1,0:T(8,128)(2,1)}), bf16[256,1024]{1,0:T(8,128)(2,1)}) %reduce-scatter.2.cloned.1.call-update) | async-done | bytes 524304 | tf_op jit(solution)/shard_map/reduce_scatter | solution.py:132
  (10 shorter events, 0.1 us)
Async XLA Ops:
  6.5 44.6 %copy-start = (bf16[4096,256]{1,0:T(8,128)(2,1)S(1)}, bf16[4096,256]{1,0:T(8,128)(2,1)}, u32[]{:S(2)}) copy-start(bf16[4096,256]{1,0:T(8,128)(2,1)} %param.19) | copy-start | bytes 6291460
  6.5 44.6 %all-gather.2.cloned.1.call-start = ((), (), s32[]{:S(2)}) async-start(), calls=%async_computation.1 | async-start | bytes 2621440 | tf_op jit(solution)/shard_map/all_gather | solution.py:85
  7.3 150.1 %reduce-scatter.2.cloned.1.call-start = ((), (), s32[]{:S(2)}) async-start(), calls=%async_computation.2 | async-start | bytes 2621440 | tf_op jit(solution)/shard_map/reduce_scatter | solution.py:132
  57.4 28.5 %collective-permute-start = (bf16[2,256,2,128]{3,1,2,0:T(8,128)(2,1)S(1)}, bf16[2,256,2,128]{3,1,2,0:T(8,128)(2,1)}, u32[]{:S(2)}, u32[]{:S(2)}) collective-permute-start(bf16[2,256,2,128]{3,1,2,0:T(8,128)(2,1)S(1)} %pad_maximum_fusion.1), channel_id=1, source_target_pairs={{0,4},{4,8},{8,12},{12,16},{16,20},{20,24},{24,28},{28,32},{32,36}... | collective-permute-start | bytes 786440 | tf_op jit(solution)/shard_map/ppermute | solution.py:15
  61.1 32.1 %collective-permute-start.1 = (bf16[2,256,2,128]{3,1,2,0:T(8,128)(2,1)S(1)}, bf16[2,256,2,128]{3,1,2,0:T(8,128)(2,1)}, u32[]{:S(2)}, u32[]{:S(2)}) collective-permute-start(bf16[2,256,2,128]{3,1,2,0:T(8,128)(2,1)S(1)} %pad_maximum_fusion.1), channel_id=1, source_target_pairs={{0,8},{4,12},{8,16},{12,20},{16,24},{20,28},{24,32},{28,36},{32,40... | collective-permute-start | bytes 786440 | tf_op jit(solution)/shard_map/ppermute | solution.py:15
  64.9 28.3 %collective-permute-start.2 = (bf16[2,256,2,128]{3,1,2,0:T(8,128)(2,1)S(1)}, bf16[2,256,2,128]{3,1,2,0:T(8,128)(2,1)}, u32[]{:S(2)}, u32[]{:S(2)}) collective-permute-start(bf16[2,256,2,128]{3,1,2,0:T(8,128)(2,1)S(1)} %pad_maximum_fusion.1), channel_id=1, source_target_pairs={{0,12},{4,16},{8,20},{12,24},{16,28},{20,32},{24,36},{28,40},{32,4... | collective-permute-start | bytes 786440 | tf_op jit(solution)/shard_map/ppermute | solution.py:15
  68.1 25.1 %collective-permute-start.3 = (bf16[2,256,2,128]{3,1,2,0:T(8,128)(2,1)S(1)}, bf16[2,256,2,128]{3,1,2,0:T(8,128)(2,1)}, u32[]{:S(2)}, u32[]{:S(2)}) collective-permute-start(bf16[2,256,2,128]{3,1,2,0:T(8,128)(2,1)S(1)} %pad_maximum_fusion.1), channel_id=1, source_target_pairs={{0,16},{4,20},{8,24},{12,28},{16,32},{20,36},{24,40},{28,44},{32,4... | collective-permute-start | bytes 786440 | tf_op jit(solution)/shard_map/ppermute | solution.py:15
Sparse Core Ops, SparseCore 0:
  9.5 41.6 all-gather.1
  104.4 52.9 reduce-scatter.1
where the time goes:
time: 165 us; the launch traced here: 164 us
  waiting for transfers between devices  87.8 us (53%)
  matrix products  26.9 us (16%)
  between operations  20.1 us (12%)
  starting transfers between devices  15 us (9%)
  other arithmetic  8.64 us (5%)
  local copies, waits for them, and re-layouts  5.73 us (3%)
    reduce_scatter x1, waiting for transfers between devices, body(): lax.psum_scatter(partial_value.astype(jnp.bfloat16), 'tp', scatter_dimens...  53.1 us
    all_gather x1, waiting for transfers between devices, body(): whole = lax.all_gather(hidden_in, 'tp', axis=1, tiled=True)  33.9 us
    ppermute x4, starting transfers between devices, passed_along(): return lax.ppermute(block, axis, route)  15 us
    dot_general x1, matrix products, body(): partial_value = jnp.dot(context, w_out, preferred_element_type=jnp.float32)  7.11 us
    dot_general x1, matrix products, body(): jnp.dot(whole, w_query, preferred_element_type=jnp.float32)  6.34 us
    dot_general x2, matrix products, update(): jnp.einsum('grqk,kgd->grqd', weights.astype(jnp.bfloat16), block[1], pref...  5.91 us
  transfers between devices with their start and end apart: 6, of which 2 were waited for; matrix products, arithmetic and copies ran while one was open for 15% of the time, Pallas kernels for 0%

commit v1 on v0

v1 whole, which is shorter than its diff:
```python
import functools
import math

import jax
import jax.numpy as jnp
import numpy as np
from jax import lax
from jax.experimental import pallas as pl
from jax.experimental.pallas import tpu as pltpu
from jax.sharding import PartitionSpec as P

HEAD = 128
CHUNKS = 4
REACH = 4
MESH = pl.DeviceIdType.MESH
F32 = jnp.float32
BF16 = jnp.bfloat16


def inverse_frequencies():
    exponent = np.arange(0, HEAD, 2, dtype=np.float32) / np.float32(HEAD)
    base = np.power(np.float32(500000.0), -exponent).astype(np.float32)
    wavelength = (2.0 * math.pi / base).astype(np.float32)
    smooth = (8192.0 / wavelength - 1.0) / 3.0
    blended = (1.0 - smooth) * base / 8.0 + smooth * base
    freq = np.where(wavelength < 2048.0, base, np.where(wavelength > 8192.0, base / 8.0, blended))
    return np.concatenate([freq, freq]).astype(np.float32)[None, :]


def layer(
    n_seq, n_tp,
    len_ref, freq_ref, hid_hbm, wq_hbm, wk_hbm, wv_hbm, wo_hbm, out_hbm,
    hid, w, wo, acc, kv, q, tab, bias, ctx,
    far_s, right_p, left_p, own_p, right_s, left_s, half_l, half_r, full_l, full_r, out_v,
    w_sem, hid_sem, near_s, near_r, fwd_s, fwd_r, kv_s, kv_r, rs_s, rs_r, out_sem,
):
    tok, dx = hid_hbm.shape
    docs = len_ref.shape[0]
    rows = tok // CHUNKS
    nkv = 2 * HEAD
    nq = wq_hbm.shape[1]
    heads = nq // HEAD
    group = heads // 2
    half = dx // 2
    seq = lax.axis_index("seq")
    x = lax.axis_index("tp")
    core = lax.rem(seq, 2)
    right = {"tp": lax.rem(x + 1, n_tp)}
    left = {"tp": lax.rem(x + n_tp - 1, n_tp)}
    ahead = {"seq": lax.rem(seq + 2, n_seq)}
    behind = {"seq": lax.rem(seq + n_seq - 2, n_seq)}
    sibling = {"seq": seq + 1 - 2 * core}

    loads = []
    shards = (x, lax.rem(x + n_tp - 1, n_tp), lax.rem(x + 1, n_tp), lax.rem(x + 2, n_tp))
    own_copy = pltpu.make_async_copy(hid_hbm, hid.at[:, pl.ds(0, dx)], hid_sem)
    own_copy.start()
    for r in range(4):
        src = pl.ds(pl.multiple_of(shards[r] * dx, dx), dx)
        dst = pl.ds(r * dx, dx)
        for k, (ref, at, width) in enumerate(
            ((wk_hbm, 0, nkv), (wv_hbm, nkv, nkv), (wq_hbm, 2 * nkv, nq))
        ):
            copy = pltpu.make_async_copy(
                ref.at[src], w.at[dst, pl.ds(at, width)], w_sem.at[3 * r + k]
            )
            copy.start()
            loads.append(copy)
    out_loads = []
    for r, shard in enumerate((shards[0], shards[2], shards[1], shards[3])):
        columns = pl.ds(pl.multiple_of(shard * dx, dx), dx)
        copy = pltpu.make_async_copy(wo_hbm.at[:, columns], wo.at[r], w_sem.at[12 + r])
        copy.start()
        out_loads.append(copy)

    barrier = pltpu.get_barrier_semaphore()
    for other in (right, left, ahead, behind, sibling):
        pl.semaphore_signal(barrier, inc=1, device_id=other, device_id_type=MESH)
    pl.semaphore_wait(barrier, 5)

    def remote(src, dst, send, recv, to):
        return pltpu.make_async_remote_copy(
            src_ref=src, dst_ref=dst, send_sem=send, recv_sem=recv,
            device_id=to, device_id_type=MESH,
        )

    def chunk(c, base=0):
        return pl.ds(base + c * rows, rows)

    def near(c):
        return (
            remote(hid_hbm.at[chunk(c)], hid.at[chunk(c), pl.ds(dx, dx)],
                   near_s.at[0, c], near_r.at[0, c], right),
            remote(hid_hbm.at[chunk(c)], hid.at[chunk(c), pl.ds(2 * dx, dx)],
                   near_s.at[1, c], near_r.at[1, c], left),
        )

    def forward(c):
        return (
            remote(hid.at[chunk(c), pl.ds(dx, half)], hid.at[chunk(c), pl.ds(3 * dx, half)],
                   fwd_s.at[0, c], fwd_r.at[0, c], right),
            remote(hid.at[chunk(c), pl.ds(2 * dx + half, half)],
                   hid.at[chunk(c), pl.ds(3 * dx + half, half)],
                   fwd_s.at[1, c], fwd_r.at[1, c], left),
        )

    def kv_rows(place, c):
        return kv.at[:, pl.ds(pl.multiple_of((place + core) * tok + c * rows, rows), rows),
                     pl.ds(0, nkv)]

    def kv_copy(kind, c):
        src, dst, to = (
            (4, 2, ahead), (2, 0, ahead), (4, 4, sibling), (2, 2, sibling), (0, 0, sibling)
        )[kind]
        return remote(kv_rows(src, c), kv_rows(dst, c), kv_s.at[kind, c], kv_r.at[kind, c], to)

    started = []

    def start(copies):
        for copy in copies:
            copy.start()
            started.append(copy)

    nears = [near(c) for c in range(CHUNKS)]
    forwards = [forward(c) for c in range(CHUNKS)]
    kvs = [[kv_copy(kind, c) for c in range(CHUNKS)] for kind in range(5)]
    start(nears[0])
    start(nears[1])

    row = lax.broadcasted_iota(jnp.int32, (tok, HEAD), 0)
    lane = lax.broadcasted_iota(jnp.int32, (tok, HEAD), 1)
    pos = row + seq * tok

    def next_doc(d, state):
        end, first = state
        end = end + len_ref[d]
        return end, jnp.where(pos >= end, end, first)

    _, first = lax.fori_loop(0, docs, next_doc, (jnp.int32(0), jnp.zeros_like(pos)))
    angle = (pos - first).astype(F32) * freq_ref[...]
    cosine = jnp.cos(angle)
    sine = jnp.where(lane < HEAD // 2, -1.0, 1.0) * jnp.sin(angle)
    scale = math.log2(math.e) / math.sqrt(HEAD)
    tab[0] = cosine
    tab[1] = sine
    tab[2] = cosine * scale
    tab[3] = sine * scale
    low = first - (seq * tok - REACH * tok)
    high = row + REACH * tok
    span = bias.shape[1]
    step = 2 * rows
    for b in range(tok // step):
        part = slice(b * step, (b + 1) * step)
        for k in range(span // HEAD):
            key = lane[part] + (b * step + k * HEAD)
            seen = (key >= low[part]) & (key <= high[part])
            bias[part, k * HEAD:(k + 1) * HEAD] = jnp.where(seen, 0.0, -1e30)
    kv[:, :, nkv:] = jnp.ones((2, kv.shape[1], HEAD), BF16)

    tile = 2 * HEAD
    tiles = w.shape[1] // tile

    def project_near(c):
        @pl.loop(0, tiles)
        def _(j):
            at = pl.ds(pl.multiple_of(j * tile, tile), tile)
            acc[chunk(c), at] = jnp.dot(
                hid[chunk(c), 0:3 * dx], w[0:3 * dx, at], preferred_element_type=F32
            )

    def far_tile(c, at):
        return acc[chunk(c), at] + jnp.dot(
            hid[chunk(c), 3 * dx:], w[3 * dx:, at], preferred_element_type=F32
        )

    def rotated(part, c, cos_at):
        return part * tab[cos_at, chunk(c)] + pltpu.roll(part, HEAD // 2, 1) * tab[cos_at + 1, chunk(c)]

    def project_far(c):
        own = pl.ds(pl.multiple_of((4 + core) * tok + c * rows, rows), rows)
        keys = far_tile(c, pl.ds(0, tile))
        values = far_tile(c, pl.ds(tile, tile))
        for g in range(2):
            part = slice(g * HEAD, (g + 1) * HEAD)
            kv[g, own, 0:HEAD] = rotated(keys[:, part], c, 0).astype(BF16)
            kv[g, own, HEAD:nkv] = values[:, part].astype(BF16)
        start([kvs[0][c], kvs[2][c]])

        @pl.loop(0, tiles - 2)
        def _(j):
            two = far_tile(c, pl.ds(pl.multiple_of((j + 2) * tile, tile), tile))
            for k in range(2):
                head = 2 * j + k
                place = pl.ds(pl.multiple_of(lax.rem(head, group) * rows, rows), rows)
                q[head // group, c, place] = rotated(
                    two[:, k * HEAD:(k + 1) * HEAD], c, 2
                ).astype(BF16)

    def pass_on(c):
        kvs[0][c].wait_recv()
        start([kvs[1][c], kvs[3][c]])

    def pass_far(c):
        kvs[1][c].wait_recv()
        start([kvs[4][c]])

    own_copy.wait()
    for c in range(CHUNKS):
        for copy in nears[c]:
            copy.wait_recv()
        start(forwards[c])
        if c + 2 < CHUNKS:
            start(nears[c + 2])
        if c == 0:
            for copy in loads[:9]:
                copy.wait()
        project_near(c)
        if c >= 1:
            if c == 1:
                for copy in loads[9:]:
                    copy.wait()
            for copy in forwards[c - 1]:
                copy.wait_recv()
            project_far(c - 1)
        if c >= 2:
            pass_on(c - 2)
        if c >= 3:
            pass_far(c - 3)
    for copy in forwards[CHUNKS - 1]:
        copy.wait_recv()
    project_far(CHUNKS - 1)
    pass_on(CHUNKS - 2)
    pass_far(CHUNKS - 3)
    pass_on(CHUNKS - 1)
    pass_far(CHUNKS - 2)
    pass_far(CHUNKS - 1)
    for kind in (2, 3, 4):
        for c in range(CHUNKS):
            kvs[kind][c].wait_recv()
    for copy in out_loads:
        copy.wait()

    def attend(c):
        first_key = (c // 2) * step
        window = pl.ds(pl.multiple_of(core * tok + first_key, step), span)
        for g in range(2):
            scores = lax.dot_general(
                q[g, c], kv[g, window, 0:HEAD], (((1,), (1,)), ((), ())),
                preferred_element_type=F32,
            )
            scores = scores.reshape(group, rows, span) + bias[chunk(c)][None]
            peak = jnp.max(scores, axis=2, keepdims=True)
            weights = jnp.exp2(scores - peak).reshape(group * rows, span).astype(BF16)
            both = jnp.dot(weights, kv[g, window, HEAD:], preferred_element_type=F32)
            value = (both[:, 0:HEAD] / both[:, HEAD:]).astype(BF16)
            for h in range(group):
                at = (g * group + h) * HEAD
                ctx[c, :, at:at + HEAD] = value[h * rows:(h + 1) * rows]

    out_tile = min(512, dx)

    def output_part(c, r, ref):
        @pl.loop(0, dx // out_tile)
        def _(j):
            at = pl.ds(pl.multiple_of(j * out_tile, out_tile), out_tile)
            ref[c, :, at] = jnp.dot(ctx[c], wo[r, :, at], preferred_element_type=F32).astype(
                ref.dtype
            )

    far_copies = [
        (
            remote(far_s.at[c, :, pl.ds(0, half)], half_l.at[c], rs_s.at[0, c], rs_r.at[0, c], right),
            remote(far_s.at[c, :, pl.ds(half, half)], half_r.at[c], rs_s.at[1, c], rs_r.at[1, c], left),
        )
        for c in range(CHUNKS)
    ]
    sum_copies = [
        (
            remote(right_s.at[c], full_l.at[c], rs_s.at[2, c], rs_r.at[2, c], right),
            remote(left_s.at[c], full_r.at[c], rs_s.at[3, c], rs_r.at[3, c], left),
        )
        for c in range(CHUNKS)
    ]

    def add_halves(c):
        far_copies[c][0].wait_recv()
        right_s[c, :, 0:half] = (right_p[c, :, 0:half] + half_l[c].astype(F32)).astype(BF16)
        right_s[c, :, half:] = right_p[c, :, half:].astype(BF16)
        start(sum_copies[c][:1])
        far_copies[c][1].wait_recv()
        left_s[c, :, 0:half] = left_p[c, :, 0:half].astype(BF16)
        left_s[c, :, half:] = (left_p[c, :, half:] + half_r[c].astype(F32)).astype(BF16)
        start(sum_copies[c][1:])

    out_copies = []

    def finish(c):
        for copy in sum_copies[c]:
            copy.wait_recv()
        out_v[c] = (own_p[c] + (full_l[c].astype(F32) + full_r[c].astype(F32))).astype(BF16)
        copy = pltpu.make_async_copy(out_v.at[c], out_hbm.at[chunk(c)], out_sem.at[c])
        copy.start()
        out_copies.append(copy)

    for c in range(CHUNKS):
        attend(c)
        output_part(c, 3, far_s)
        start(far_copies[c])
        if c >= 1:
            add_halves(c - 1)
        output_part(c, 1, right_p)
        output_part(c, 2, left_p)
        output_part(c, 0, own_p)
        if c >= 2:
            finish(c - 2)
    add_halves(CHUNKS - 1)
    finish(CHUNKS - 2)
    finish(CHUNKS - 1)
    for copy in started:
        copy.wait_send()
    for copy in out_copies:
        copy.wait()


def body(n_seq, n_tp, hidden_in, doc_lengths, w_query, w_key, w_value, w_out):
    tok, dx = hidden_in.shape
    rows = tok // CHUNKS
    nq = w_query.shape[1]
    wide = w_key.shape[1] + w_value.shape[1] + nq
    span = REACH * tok + 2 * rows
    group = nq // HEAD // 2
    anywhere = pl.BlockSpec(memory_space=pl.ANY)
    dma = pltpu.SemaphoreType.DMA
    part = (CHUNKS, rows, dx)
    return pl.pallas_call(
        functools.partial(layer, n_seq, n_tp),
        out_shape=jax.ShapeDtypeStruct((tok, dx), BF16),
        in_specs=[pl.BlockSpec(memory_space=pltpu.SMEM), pl.BlockSpec(memory_space=pltpu.VMEM)]
        + [anywhere] * 5,
        out_specs=anywhere,
        scratch_shapes=[
            pltpu.VMEM((tok, 4 * dx), BF16),
            pltpu.VMEM((4 * dx, wide), BF16),
            pltpu.VMEM((4, nq, dx), BF16),
            pltpu.VMEM((tok, wide), F32),
            pltpu.VMEM((2, 6 * tok, 3 * HEAD), BF16),
            pltpu.VMEM((2, CHUNKS, group * rows, HEAD), BF16),
            pltpu.VMEM((4, tok, HEAD), F32),
            pltpu.VMEM((tok, span), F32),
            pltpu.VMEM((CHUNKS, rows, nq), BF16),
            pltpu.VMEM(part, BF16),
            pltpu.VMEM(part, F32),
            pltpu.VMEM(part, F32),
            pltpu.VMEM(part, F32),
            pltpu.VMEM(part, BF16),
            pltpu.VMEM(part, BF16),
            pltpu.VMEM((CHUNKS, rows, dx // 2), BF16),
            pltpu.VMEM((CHUNKS, rows, dx // 2), BF16),
            pltpu.VMEM(part, BF16),
            pltpu.VMEM(part, BF16),
            pltpu.VMEM(part, BF16),
            dma((16,)),
            dma(()),
            dma((2, CHUNKS)),
            dma((2, CHUNKS)),
            dma((2, CHUNKS)),
            dma((2, CHUNKS)),
            dma((5, CHUNKS)),
            dma((5, CHUNKS)),
            dma((4, CHUNKS)),
            dma((4, CHUNKS)),
            dma((CHUNKS,)),
        ],
        compiler_params=pltpu.CompilerParams(
            collective_id=0, has_side_effects=True, vmem_limit_bytes=58 * 2**20
        ),
        cost_estimate=pl.CostEstimate(
            flops=7 * 10**9, bytes_accessed=22 * 10**6, transcendentals=2 * 10**6
        ),
        name="layer",
    )(doc_lengths, jnp.asarray(inverse_frequencies()), hidden_in, w_query, w_key, w_value, w_out)


def solution(mesh):
    return jax.shard_map(
        functools.partial(body, mesh.shape["seq"], mesh.shape["tp"]),
        mesh=mesh,
        in_specs=(P("seq", "tp"), P(), P(None, "tp"), P(None, "tp"), P(None, "tp"), P("tp", None)),
        out_specs=P("seq", "tp"),
        check_vma=False,
    )
```

time: 165 us -> 74 us (0.45)
  waiting for transfers between devices: 87.8 us -> 0 us
  Pallas kernels: 0 us -> 72 us
  matrix products: 26.9 us -> 0 us
  between operations: 20.1 us -> 0.01 us
  starting transfers between devices: 15 us -> 0 us
  other arithmetic: 8.64 us -> 0 us
  local copies, waits for them, and re-layouts: 5.73 us -> 1.87 us
    pallas_call x0 -> x1, Pallas kernels: none -> 72 us  [body(): pl.pallas_call(functools.partial(layer, n_seq, n_tp), out_shape=jax.Shape...]
    reduce_scatter x1 -> x0, waiting for transfers between devices: 53.1 us -> none  [body(): lax.psum_scatter(partial_value.astype(jnp.bfloat16), 'tp', scatter_dimens...]
    all_gather x1 -> x0, waiting for transfers between devices: 33.9 us -> none  [body(): whole = lax.all_gather(hidden_in, 'tp', axis=1, tiled=True)]
    dot_general x8 -> x0, matrix products: 26.9 us -> none  [the longest x1 7.11 us: body(): partial_value = jnp.dot(context, w_out, preferred_element_type=jnp.float32)]
    ppermute x4 -> x0, starting transfers between devices: 15 us -> none  [passed_along(): return lax.ppermute(block, axis, route)]
    cond x2 -> x0, local copies, waits for them, and re-layouts: 3.14 us -> none  [the longest x1 2.55 us: attend_block(): return lax.cond(needed, update, unchanged, running)]
    reduce_sum x3 -> x0, other arithmetic: 2.5 us -> none  [the longest x2 1.74 us: update(): total = total * factor + jnp.sum(weights, axis=-1)]
  transfers between devices with their start and end apart: 6 -> 0, of which waited for: 2 -> 0; matrix products, arithmetic and copies ran while one was open for 15% -> 0% of each run, Pallas kernels for 0% -> 0%
where the time goes in v1:
time: 74 us; the launch traced here: 73.9 us
  Pallas kernels  72 us (97%)
  local copies, waits for them, and re-layouts  1.87 us (3%)
    pallas_call x1, Pallas kernels, body(): pl.pallas_call(functools.partial(layer, n_seq, n_tp), out_shape=jax.Shape...  72 us
    unnamed x1, local copies, waits for them, and re-layouts  1.87 us

profile of v1, /device:TPU:1, one launch (start us, length us, event | category | flops | bytes accessed | tf_op | source)
XLA Modules:
  0.0 73.9 jit_solution(6167844834791688020)
XLA Ops:
  0.0 72.0 %layer.1 = bf16[256,1024]{1,0:T(8,128)(2,1)} custom-call(s32[64]{0:T(128)} %len_ref.1, f32[1,128]{1,0:T(1,128)} %constant.2.clone.freq_ref, bf16[256,1024]{1,0:T(8,128)(2,1)} %hid_hbm.1, bf16[4096,1024]{1,0:T(8,128)(2,1)} %wq_hbm.1, bf16[4096,256]{1,0:T(8,128)(2,1)} %wk_hbm.1, bf16[4096,256]{1,0:T(8,128)(2,1)} %wv_hbm.1, bf16[1024,4096]{1,0:T(8,128)(2,1)} %wo_hbm.1), custom_call_target="tpu_custom_call" | custom-call | flops 7000000000 | bytes 22000000 | tf_op jit(solution)/shard_map/layer/pallas_call | solution.py:335
  72.0 1.9 %copy.9 = bf16[256,1024]{1,0:T(8,128)(2,1)} copy(bf16[256,1024]{1,0:T(8,128)(2,1)} %layer.1) | data formatting | bytes 1048576

commit v2 on v0

v2 whole, which is shorter than its diff:
```python
import functools
import math

import jax
import jax.numpy as jnp
import numpy as np
from jax import lax
from jax.experimental import pallas as pl
from jax.experimental.pallas import tpu as pltpu
from jax.sharding import PartitionSpec as P

HEAD = 128
REACH = 4
GATHER = ((64, False, "pass"), (64, False, "pass"), (64, False, "pass"), (64, False, "two"))
SCATTER = ((64, False), (64, False), (64, False), (64, False))
SPAN = 1152
EARLY = 2
MESH = pl.DeviceIdType.MESH
F32 = jnp.float32
BF16 = jnp.bfloat16
OFF = frozenset()


def inverse_frequencies():
    exponent = np.arange(0, HEAD, 2, dtype=np.float32) / np.float32(HEAD)
    base = np.power(np.float32(500000.0), -exponent).astype(np.float32)
    wavelength = (2.0 * math.pi / base).astype(np.float32)
    smooth = (8192.0 / wavelength - 1.0) / 3.0
    blended = (1.0 - smooth) * base / 8.0 + smooth * base
    freq = np.where(wavelength < 2048.0, base, np.where(wavelength > 8192.0, base / 8.0, blended))
    return np.concatenate([freq, freq]).astype(np.float32)[None, :]


def bounds(chunks):
    at, out = 0, []
    for size in chunks:
        out.append((at, size))
        at += size
    return out


class Move:
    def __init__(self, copy, sends=None, lands=None):
        self.copy, self.sends, self.lands = copy, sends, lands

    @staticmethod
    def on(condition, act):
        if condition is None:
            act()
        else:
            pl.when(condition)(act)

    def start(self):
        self.on(self.sends, self.copy.start)

    def sent(self):
        self.on(self.sends, self.copy.wait_send)

    def landed(self):
        self.on(self.lands, self.copy.wait_recv)


class Nothing:
    def start(self):
        pass

    sent = landed = start


def layer(
    n_seq, n_tp,
    len_ref, freq_ref, hid_hbm, wq_hbm, wk_hbm, wv_hbm, wo_hbm, out_v,
    hid, w, wo, acc, kv, q, tab, bias, ctx,
    far_s, right_p, left_p, own_p, right_s, left_s, half_l, half_r, full_l, full_r, full_o,
    w_sem, hid_sem, near_s, near_r, fwd_s, fwd_r, kv_s, kv_r, rs_s, rs_r,
):
    tok, dx = hid_hbm.shape
    docs = len_ref.shape[0]
    nkv = 2 * HEAD
    nq = wq_hbm.shape[1]
    group = nq // HEAD // 2
    half = dx // 2
    seq = lax.axis_index("seq")
    x = lax.axis_index("tp")
    core = lax.rem(seq, 2)
    right = {"tp": lax.rem(x + 1, n_tp)}
    left = {"tp": lax.rem(x + n_tp - 1, n_tp)}
    across = {"tp": lax.rem(x + 2, n_tp)}
    sibling = {"seq": seq + 1 - 2 * core}
    ahead, ahead2, behind, behind2 = ({"seq": seq + d} for d in (2, 4, -2, -4))
    has_ahead, has_ahead2 = seq + 2 < n_seq, seq + 4 < n_seq
    has_behind, has_behind2 = seq >= 2, seq >= 4
    gather = bounds([c[0] for c in GATHER])
    scatter = bounds([c[0] for c in SCATTER])

    @pl.when(seq < 4)
    def _():
        kv[:, 0:4 * tok] = jnp.zeros((2, 4 * tok, 3 * HEAD), BF16)

    @pl.when(core == 0)
    def _():
        kv[:, 5 * tok:6 * tok, 0:nkv] = jnp.zeros((2, tok, nkv), BF16)

    barrier = pltpu.get_barrier_semaphore()

    def greet(other):
        pl.semaphore_signal(barrier, inc=1, device_id=other, device_id_type=MESH)

    for other in (right, left, across, sibling):
        greet(other)
    for other, there in (
        (ahead, has_ahead), (behind, has_behind), (ahead2, has_ahead2), (behind2, has_behind2)
    ):
        pl.when(there)(functools.partial(greet, other))

    shards = (x, lax.rem(x + n_tp - 1, n_tp), lax.rem(x + 1, n_tp), lax.rem(x + 2, n_tp))
    own_copy = pltpu.make_async_copy(hid_hbm, hid.at[:, pl.ds(0, dx)], hid_sem)
    own_copy.start()
    loads = {}

    def load(name, index, src, dst):
        copy = pltpu.make_async_copy(src, dst, w_sem.at[index])
        copy.start()
        loads.setdefault(name, []).append(copy)

    def load_keys(r):
        src = pl.ds(pl.multiple_of(shards[r] * dx, dx), dx)
        dst = pl.ds(r * dx, dx)
        name = "far" if r == 3 else "near"
        load(name, 3 * r, wk_hbm.at[src], w.at[dst, pl.ds(0, nkv)])
        load(name, 3 * r + 1, wv_hbm.at[src], w.at[dst, pl.ds(nkv, nkv)])

    load_keys(0)
    row = lax.broadcasted_iota(jnp.int32, (tok, HEAD), 0)
    lane = lax.broadcasted_iota(jnp.int32, (tok, HEAD), 1)
    pos = row + seq * tok

    def next_doc(d, state):
        end, first = state
        end = end + len_ref[d]
        return end, jnp.where(pos >= end, end, first)

    _, first = lax.fori_loop(0, docs, next_doc, (jnp.int32(0), jnp.zeros_like(pos)))
    angle = (pos - first).astype(F32) * freq_ref[...]
    cosine = jnp.cos(angle)
    sine = jnp.where(lane < HEAD // 2, -1.0, 1.0) * jnp.sin(angle)
    scale = math.log2(math.e) / math.sqrt(HEAD)
    tab[0] = cosine
    tab[1] = sine
    tab[2] = cosine * scale
    tab[3] = sine * scale
    low = first - (seq * tok - REACH * tok)
    high = row + REACH * tok
    for at, size in scatter:
        part = slice(at, at + size)
        for k in range(SPAN // HEAD):
            key = lane[part] + (at + k * HEAD)
            seen = (key >= low[part]) & (key <= high[part])
            bias[part, k * HEAD:(k + 1) * HEAD] = jnp.where(seen, 0.0, -1e30)
    kv[:, :, nkv:] = jnp.ones((2, kv.shape[1], HEAD), BF16)
    kv[:, 6 * tok:, 0:nkv] = jnp.zeros((2, kv.shape[1] - 6 * tok, nkv), BF16)

    others = 4
    for there in (has_ahead, has_behind, has_ahead2, has_behind2):
        others = others + jnp.where(there, 1, 0)
    pl.semaphore_wait(barrier, others)

    def remote(src, dst, send, recv, to, sends=None, lands=None, kind=""):
        if kind in OFF:
            return Nothing()
        copy = pltpu.make_async_remote_copy(
            src_ref=src, dst_ref=dst, send_sem=send, recv_sem=recv,
            device_id=to, device_id_type=MESH,
        )
        return Move(copy, sends, lands)

    def near(c):
        at = pl.ds(*gather[c])
        moves = [
            remote(hid_hbm.at[at], hid.at[at, pl.ds(dx, dx)],
                   near_s.at[0, c], near_r.at[0, c], right, kind="ag"),
            remote(hid_hbm.at[at], hid.at[at, pl.ds(2 * dx, dx)],
                   near_s.at[1, c], near_r.at[1, c], left, kind="ag"),
        ]
        return moves

    def far(c):
        at = pl.ds(*gather[c])
        if GATHER[c][1]:
            return [remote(hid_hbm.at[at], hid.at[at, pl.ds(3 * dx, dx)],
                           fwd_s.at[0, c], fwd_r.at[0, c], across, kind="ag")]
        return [
            remote(hid.at[at, pl.ds(dx, half)], hid.at[at, pl.ds(3 * dx, half)],
                   fwd_s.at[0, c], fwd_r.at[0, c], right, kind="ag"),
            remote(hid.at[at, pl.ds(2 * dx + half, half)],
                   hid.at[at, pl.ds(3 * dx + half, half)],
                   fwd_s.at[1, c], fwd_r.at[1, c], left, kind="ag"),
        ]

    def place(block, c):
        first, size = gather[c]
        return pl.ds(pl.multiple_of((block + core) * tok + first, 16), size)

    def kv_move(kind, c):
        passes = GATHER[c][2] == "pass"
        first_core, second_core = core == 0, core == 1
        src, dst, to, sends, lands = (
            (4, 2, ahead, has_ahead, has_behind),
            (2, 0, ahead, has_ahead & has_behind, has_behind2) if passes
            else (4, 0, ahead2, has_ahead2, has_behind2),
            (4, 4, sibling, first_core, second_core),
            (2, 2, sibling, has_behind, has_behind),
            (0, 0, sibling, has_behind2 & second_core, has_behind2 & first_core),
        )[kind]
        return remote(
            kv.at[:, place(src, c), pl.ds(0, nkv)], kv.at[:, place(dst, c), pl.ds(0, nkv)],
            kv_s.at[kind, c], kv_r.at[kind, c], to, sends, lands, kind="kvx",
        )

    started = []

    def start(moves):
        for move in moves:
            move.start()
            started.append(move)

    def landed(moves):
        for move in moves:
            move.landed()

    count = len(GATHER)
    nears = [near(c) for c in range(count)]
    fars = [far(c) for c in range(count)]
    kvs = [[kv_move(kind, c) for c in range(count)] for kind in range(5)]
    def start_near(c):
        start(nears[c])
        if GATHER[c][1]:
            start(fars[c])

    for c in range(min(EARLY, count)):
        start_near(c)
    for r in (1, 2, 3):
        load_keys(r)
    for r in range(4):
        src = pl.ds(pl.multiple_of(shards[r] * dx, dx), dx)
        load("q", 3 * r + 2, wq_hbm.at[src], w.at[pl.ds(r * dx, dx), pl.ds(2 * nkv, nq)])
    for r, shard in enumerate((shards[0], shards[2], shards[1], shards[3])):
        columns = pl.ds(pl.multiple_of(shard * dx, dx), dx)
        load("out", 12 + r, wo_hbm.at[:, columns], wo.at[r])

    def near_keys(c):
        if "qkv" in OFF:
            return
        at = pl.ds(*gather[c])
        acc[at] = jnp.dot(hid[at, 0:3 * dx], w[0:3 * dx, 0:2 * nkv], preferred_element_type=F32)

    def rotated(part, at, which):
        return part * tab[which, at] + pltpu.roll(part, HEAD // 2, 1) * tab[which + 1, at]

    def far_keys(c):
        at = pl.ds(*gather[c])
        own = place(4, c)
        if "qkv" not in OFF:
            both = acc[at] + jnp.dot(
                hid[at, 3 * dx:], w[3 * dx:, 0:2 * nkv], preferred_element_type=F32
            )
            for g in range(2):
                one = slice(g * HEAD, (g + 1) * HEAD)
                kv[g, own, 0:HEAD] = rotated(both[:, one], at, 0).astype(BF16)
                kv[g, own, HEAD:nkv] = both[:, nkv + g * HEAD:nkv + (g + 1) * HEAD].astype(BF16)
        start([kvs[0][c], kvs[2][c]])
        if GATHER[c][2] == "two":
            start([kvs[1][c]])

    def pass_on(c):
        landed([kvs[0][c]])
        if GATHER[c][2] == "pass":
            start([kvs[1][c]])
        start([kvs[3][c]])

    def pass_far(c):
        landed([kvs[1][c]])
        start([kvs[4][c]])

    def project_queries(j):
        if "qkv" in OFF:
            return
        at = pl.ds(0, tok)
        two = jnp.dot(
            hid[...], w[:, 2 * nkv + 2 * j * HEAD:2 * nkv + 2 * (j + 1) * HEAD],
            preferred_element_type=F32,
        )
        for k in range(2):
            q[2 * j + k] = rotated(two[:, k * HEAD:(k + 1) * HEAD], at, 2).astype(BF16)

    def loaded(name):
        for copy in loads[name]:
            copy.wait()

    own_copy.wait()
    for c in range(count):
        landed(nears[c])
        if not GATHER[c][1]:
            start(fars[c])
        if c + EARLY < count:
            start_near(c + EARLY)
        if c == 0:
            loaded("near")
        near_keys(c)
        if c >= 1:
            if c == 1:
                loaded("far")
            landed(fars[c - 1])
            far_keys(c - 1)
        if c >= 2:
            pass_on(c - 2)
        if c >= 3:
            pass_far(c - 3)
    landed(fars[count - 1])
    far_keys(count - 1)
    loaded("q")
    pass_on(count - 2)
    pass_far(count - 3)
    project_queries(0)
    project_queries(1)
    pass_far(count - 2)
    project_queries(2)
    pass_on(count - 1)
    project_queries(3)
    pass_far(count - 1)
    loaded("out")
    for kind in (2, 3, 4):
        landed(kvs[kind])

    def attend(c):
        if "att" in OFF:
            return
        first, size = scatter[c]
        at = pl.ds(first, size)
        window = pl.ds(pl.multiple_of(core * tok + first, 16), SPAN)
        for g in range(2):
            mine = q[g * group:(g + 1) * group, at].reshape(group * size, HEAD)
            scores = lax.dot_general(
                mine, kv[g, window, 0:HEAD], (((1,), (1,)), ((), ())), preferred_element_type=F32
            )
            scores = scores.reshape(group, size, SPAN) + bias[at][None]
            peak = jnp.max(scores, axis=2, keepdims=True)
            weights = jnp.exp2(scores - peak).reshape(group * size, SPAN).astype(BF16)
            both = jnp.dot(weights, kv[g, window, HEAD:], preferred_element_type=F32)
            value = (both[:, 0:HEAD] / both[:, HEAD:]).astype(BF16)
            for h in range(group):
                to = (g * group + h) * HEAD
                ctx[at, to:to + HEAD] = value[h * size:(h + 1) * size]

    def output_part(c, r, ref):
        if "proj" in OFF:
            return
        at = pl.ds(*scatter[c])
        ref[at] = jnp.dot(ctx[at], wo[r], preferred_element_type=F32).astype(ref.dtype)

    def far_moves(c):
        at = pl.ds(*scatter[c])
        if SCATTER[c][1]:
            return [remote(far_s.at[at], full_o.at[at], rs_s.at[0, c], rs_r.at[0, c], across, kind="rs")]
        return [
            remote(far_s.at[at, pl.ds(0, half)], half_l.at[at],
                   rs_s.at[0, c], rs_r.at[0, c], right, kind="rs"),
            remote(far_s.at[at, pl.ds(half, half)], half_r.at[at],
                   rs_s.at[1, c], rs_r.at[1, c], left, kind="rs"),
        ]

    def sum_moves(c):
        at = pl.ds(*scatter[c])
        return [
            remote(right_s.at[at], full_l.at[at], rs_s.at[2, c], rs_r.at[2, c], right, kind="rs"),
            remote(left_s.at[at], full_r.at[at], rs_s.at[3, c], rs_r.at[3, c], left, kind="rs"),
        ]

    parts = len(SCATTER)
    far_copies = [far_moves(c) for c in range(parts)]
    sum_copies = [sum_moves(c) for c in range(parts)]

    def add_halves(c):
        at = pl.ds(*scatter[c])
        landed(far_copies[c][:1])
        right_s[at, 0:half] = (right_p[at, 0:half] + half_l[at].astype(F32)).astype(BF16)
        right_s[at, half:] = right_p[at, half:].astype(BF16)
        start(sum_copies[c][:1])
        landed(far_copies[c][1:])
        left_s[at, 0:half] = left_p[at, 0:half].astype(BF16)
        left_s[at, half:] = (left_p[at, half:] + half_r[at].astype(F32)).astype(BF16)
        start(sum_copies[c][1:])

    def finish(c):
        at = pl.ds(*scatter[c])
        landed(sum_copies[c])
        total = full_l[at].astype(F32) + full_r[at].astype(F32)
        if SCATTER[c][1]:
            landed(far_copies[c])
            total = total + full_o[at].astype(F32)
        out_v[at] = (own_p[at] + total).astype(BF16)

    for c in range(parts):
        attend(c)
        output_part(c, 3, far_s)
        start(far_copies[c])
        if c >= 1 and not SCATTER[c - 1][1]:
            add_halves(c - 1)
        if SCATTER[c][1]:
            output_part(c, 1, right_s)
            start(sum_copies[c][:1])
            output_part(c, 2, left_s)
            start(sum_copies[c][1:])
        else:
            output_part(c, 1, right_p)
            output_part(c, 2, left_p)
        output_part(c, 0, own_p)
        if c >= 2:
            finish(c - 2)
    if not SCATTER[-1][1]:
        add_halves(parts - 1)
    finish(parts - 2)
    finish(parts - 1)
    for move in started:
        move.sent()


def body(n_seq, n_tp, hidden_in, doc_lengths, w_query, w_key, w_value, w_out):
    tok, dx = hidden_in.shape
    nq = w_query.shape[1]
    nkv = w_key.shape[1]
    anywhere = pl.BlockSpec(memory_space=pl.ANY)
    dma = pltpu.SemaphoreType.DMA
    count, parts = len(GATHER), len(SCATTER)
    return pl.pallas_call(
        functools.partial(layer, n_seq, n_tp),
        out_shape=pltpu.VMEM((tok, dx), BF16),
        in_specs=[pl.BlockSpec(memory_space=pltpu.SMEM), pl.BlockSpec(memory_space=pltpu.VMEM)]
        + [anywhere] * 5,
        out_specs=pl.BlockSpec(memory_space=pltpu.VMEM),
        scratch_shapes=[
            pltpu.VMEM((tok, 4 * dx), BF16),
            pltpu.VMEM((4 * dx, 2 * nkv + nq), BF16),
            pltpu.VMEM((4, nq, dx), BF16),
            pltpu.VMEM((tok, 2 * nkv), F32),
            pltpu.VMEM((2, 6 * tok + HEAD, 3 * HEAD), BF16),
            pltpu.VMEM((nq // HEAD, tok, HEAD), BF16),
            pltpu.VMEM((4, tok, HEAD), F32),
            pltpu.VMEM((tok, SPAN), F32),
            pltpu.VMEM((tok, nq), BF16),
            pltpu.VMEM((tok, dx), BF16),
            pltpu.VMEM((tok, dx), F32),
            pltpu.VMEM((tok, dx), F32),
            pltpu.VMEM((tok, dx), F32),
            pltpu.VMEM((tok, dx), BF16),
            pltpu.VMEM((tok, dx), BF16),
            pltpu.VMEM((tok, dx // 2), BF16),
            pltpu.VMEM((tok, dx // 2), BF16),
            pltpu.VMEM((tok, dx), BF16),
            pltpu.VMEM((tok, dx), BF16),
            pltpu.VMEM((tok, dx), BF16),
            dma((16,)),
            dma(()),
            dma((2, count)),
            dma((2, count)),
            dma((2, count)),
            dma((2, count)),
            dma((5, count)),
            dma((5, count)),
            dma((4, parts)),
            dma((4, parts)),
        ],
        compiler_params=pltpu.CompilerParams(
            collective_id=0, has_side_effects=True, vmem_limit_bytes=58 * 2**20
        ),
        cost_estimate=pl.CostEstimate(
            flops=7 * 10**9, bytes_accessed=22 * 10**6, transcendentals=2 * 10**6
        ),
        name="layer",
    )(doc_lengths, jnp.asarray(inverse_frequencies()), hidden_in, w_query, w_key, w_value, w_out)


def solution(mesh):
    return jax.shard_map(
        functools.partial(body, mesh.shape["seq"], mesh.shape["tp"]),
        mesh=mesh,
        in_specs=(P("seq", "tp"), P(), P(None, "tp"), P(None, "tp"), P(None, "tp"), P("tp", None)),
        out_specs=P("seq", "tp"),
        check_vma=False,
    )
```

time: 165 us -> 62.8 us (0.38)
  the two profiles are of different devices: /device:TPU:1 before, /device:TPU:256 now
where the time goes in v2:
time: 62.8 us; the launch traced here: 62.7 us
  Pallas kernels  61.9 us (99%)
  local copies, waits for them, and re-layouts  0.8 us (1%)
    pallas_call x1, Pallas kernels, body(): pl.pallas_call(functools.partial(layer, n_seq, n_tp), out_shape=pltpu.VME...  61.9 us

profile of v2, /device:TPU:256, one launch (start us, length us, event | category | flops | bytes accessed | tf_op | source)
XLA Modules:
  0.0 62.7 jit_solution(12979149065647038423)
XLA Ops:
  0.0 61.9 %layer.1 = bf16[256,1024]{1,0:T(8,128)(2,1)S(1)} custom-call(s32[64]{0:T(128)} %len_ref.1, f32[1,128]{1,0:T(1,128)} %constant.2.clone.freq_ref, bf16[256,1024]{1,0:T(8,128)(2,1)} %hid_hbm.1, bf16[4096,1024]{1,0:T(8,128)(2,1)} %wq_hbm.1, bf16[4096,256]{1,0:T(8,128)(2,1)} %wk_hbm.1, bf16[4096,256]{1,0:T(8,128)(2,1)} %wv_hbm.1, bf16[1024,4096]{1,0:T(8,128)(2,1)} %wo_hbm.1), custom_call_target="tpu_custom_call" | custom-call | flops 7000000000 | bytes 22000000 | tf_op jit(solution)/shard_map/layer/pallas_call | solution.py:435
  61.9 0.8 %copy.9 = bf16[256,1024]{1,0:T(8,128)(2,1)} copy(bf16[256,1024]{1,0:T(8,128)(2,1)S(1)} %layer.1) | data formatting | bytes 1048576

commit v3 on v2

--- a/solution.py
+++ b/solution.py
@@ -414,11 +414,13 @@
         else:
             output_part(c, 1, right_p)
             output_part(c, 2, left_p)
-        output_part(c, 0, own_p)
+        if c >= 1:
+            output_part(c - 1, 0, own_p)
         if c >= 2:
             finish(c - 2)
     if not SCATTER[-1][1]:
         add_halves(parts - 1)
+    output_part(parts - 1, 0, own_p)
     finish(parts - 2)
     finish(parts - 1)
     for move in started:

time: 62.8 us -> 62.5 us (level)
  no operation moved by 1% of the time
where the time goes in v3:
time: 62.5 us; the launch traced here: 62.3 us
  Pallas kernels  61.5 us (98%)
  local copies, waits for them, and re-layouts  0.8 us (1%)
    pallas_call x1, Pallas kernels, body(): pl.pallas_call(functools.partial(layer, n_seq, n_tp), out_shape=pltpu.VME...  61.5 us

profile of v3, /device:TPU:256, one launch (start us, length us, event | category | flops | bytes accessed | tf_op | source)
XLA Modules:
  0.0 62.3 jit_solution(5732820454554162934)
XLA Ops:
  0.0 61.5 %layer.1 = bf16[256,1024]{1,0:T(8,128)(2,1)S(1)} custom-call(s32[64]{0:T(128)} %len_ref.1, f32[1,128]{1,0:T(1,128)} %constant.2.clone.freq_ref, bf16[256,1024]{1,0:T(8,128)(2,1)} %hid_hbm.1, bf16[4096,1024]{1,0:T(8,128)(2,1)} %wq_hbm.1, bf16[4096,256]{1,0:T(8,128)(2,1)} %wk_hbm.1, bf16[4096,256]{1,0:T(8,128)(2,1)} %wv_hbm.1, bf16[1024,4096]{1,0:T(8,128)(2,1)} %wo_hbm.1), custom_call_target="tpu_custom_call" | custom-call | flops 7000000000 | bytes 22000000 | tf_op jit(solution)/shard_map/layer/pallas_call | solution.py:437
  61.5 0.8 %copy.9 = bf16[256,1024]{1,0:T(8,128)(2,1)} copy(bf16[256,1024]{1,0:T(8,128)(2,1)S(1)} %layer.1) | data formatting | bytes 1048576

commit v4 on v3

--- a/solution.py
+++ b/solution.py
@@ -11,10 +11,18 @@
 
 HEAD = 128
 REACH = 4
-GATHER = ((64, False, "pass"), (64, False, "pass"), (64, False, "pass"), (64, False, "two"))
+GATHER = ((32, False, "pass"), (48, False, "pass"), (48, False, "pass"), (48, False, "pass"), (48, False, "pass"), (32, False, "two"))
+ORDER = (
+    ("send", 0), ("send", 1), ("send", 2), ("send", 3), ("near", 0), ("sum", 0),
+    ("near", 1), ("sum", 1), ("near", 2), ("near", 3), ("sum", 3), ("send", 4),
+    ("far", 0), ("send", 5), ("far", 1), ("sum", 2), ("far", 2), ("far", 3),
+    ("pass", 0), ("near", 4), ("pass", 1), ("sum", 4), ("near", 5), ("pass", 2),
+    ("sum", 5), ("pass", 3), ("far", 4), ("share", 0), ("share", 1), ("far", 5),
+    ("pass", 4), ("query", 1), ("query", 3), ("share", 2), ("share", 3), ("query", 2),
+    ("pass", 5), ("share", 4), ("share", 5), ("query", 0),
+)
 SCATTER = ((64, False), (64, False), (64, False), (64, False))
 SPAN = 1152
-EARLY = 2
 MESH = pl.DeviceIdType.MESH
 F32 = jnp.float32
 BF16 = jnp.bfloat16
@@ -232,13 +240,15 @@
     nears = [near(c) for c in range(count)]
     fars = [far(c) for c in range(count)]
     kvs = [[kv_move(kind, c) for c in range(count)] for kind in range(5)]
+    order = list(ORDER)
+
     def start_near(c):
         start(nears[c])
         if GATHER[c][1]:
             start(fars[c])
 
-    for c in range(min(EARLY, count)):
-        start_near(c)
+    while order and order[0][0] == "send":
+        start_near(order.pop(0)[1])
     for r in (1, 2, 3):
         load_keys(r)
     for r in range(4):
@@ -297,37 +307,25 @@
         for copy in loads[name]:
             copy.wait()
 
-    own_copy.wait()
-    for c in range(count):
+    def wait_near(c):
         landed(nears[c])
         if not GATHER[c][1]:
             start(fars[c])
-        if c + EARLY < count:
-            start_near(c + EARLY)
-        if c == 0:
-            loaded("near")
-        near_keys(c)
-        if c >= 1:
-            if c == 1:
-                loaded("far")
-            landed(fars[c - 1])
-            far_keys(c - 1)
-        if c >= 2:
-            pass_on(c - 2)
-        if c >= 3:
-            pass_far(c - 3)
-    landed(fars[count - 1])
-    far_keys(count - 1)
-    loaded("q")
-    pass_on(count - 2)
-    pass_far(count - 3)
-    project_queries(0)
-    project_queries(1)
-    pass_far(count - 2)
-    project_queries(2)
-    pass_on(count - 1)
-    project_queries(3)
-    pass_far(count - 1)
+
+    def wait_far(c):
+        landed(fars[c])
+        far_keys(c)
+
+    steps = {
+        "send": start_near, "near": wait_near, "sum": near_keys, "far": wait_far,
+        "pass": pass_on, "share": pass_far, "query": project_queries,
+    }
+    needs = {"sum": "near", "far": "far", "query": "q"}
+    own_copy.wait()
+    for step, index in order:
+        if step in needs:
+            loaded(needs.pop(step))
+        steps[step](index)
     loaded("out")
     for kind in (2, 3, 4):
         landed(kvs[kind])

time: 62.5 us -> 60.9 us (0.974)
  the two profiles are of different devices: /device:TPU:256 before, /device:TPU:8 now
where the time goes in v4:
time: 60.9 us; the launch traced here: 60.8 us
  Pallas kernels  60 us (99%)
  local copies, waits for them, and re-layouts  0.8 us (1%)
    pallas_call x1, Pallas kernels, body(): pl.pallas_call(functools.partial(layer, n_seq, n_tp), out_shape=pltpu.VME...  60 us

profile of v4, /device:TPU:8, one launch (start us, length us, event | category | flops | bytes accessed | tf_op | source)
XLA Modules:
  0.0 60.8 jit_solution(6995087619673028866)
XLA Ops:
  0.0 60.0 %layer.1 = bf16[256,1024]{1,0:T(8,128)(2,1)S(1)} custom-call(s32[64]{0:T(128)} %len_ref.1, f32[1,128]{1,0:T(1,128)} %constant.2.clone.freq_ref, bf16[256,1024]{1,0:T(8,128)(2,1)} %hid_hbm.1, bf16[4096,1024]{1,0:T(8,128)(2,1)} %wq_hbm.1, bf16[4096,256]{1,0:T(8,128)(2,1)} %wk_hbm.1, bf16[4096,256]{1,0:T(8,128)(2,1)} %wv_hbm.1, bf16[1024,4096]{1,0:T(8,128)(2,1)} %wo_hbm.1), custom_call_target="tpu_custom_call" | custom-call | flops 7000000000 | bytes 22000000 | tf_op jit(solution)/shard_map/layer/pallas_call | solution.py:435
  60.0 0.8 %copy.9 = bf16[256,1024]{1,0:T(8,128)(2,1)} copy(bf16[256,1024]{1,0:T(8,128)(2,1)S(1)} %layer.1) | data formatting | bytes 1048576

commit v5 on v4

--- a/solution.py
+++ b/solution.py
@@ -21,7 +21,14 @@
     ("pass", 4), ("query", 1), ("query", 3), ("share", 2), ("share", 3), ("query", 2),
     ("pass", 5), ("share", 4), ("share", 5), ("query", 0),
 )
-SCATTER = ((64, False), (64, False), (64, False), (64, False))
+SCATTER = ((64, False), (80, False), (64, False), (48, False))
+SCATTER_ORDER = (
+    ("attend", 2), ("far", 2), ("attend", 1), ("far", 1), ("attend", 0), ("far", 0),
+    ("left", 2), ("right", 2), ("add", 2), ("right", 1), ("attend", 3), ("right", 3),
+    ("far", 3), ("left", 0), ("right", 0), ("add", 0), ("own", 3), ("own", 2),
+    ("left", 1), ("left", 3), ("add", 1), ("finish", 2), ("own", 1), ("own", 0),
+    ("finish", 0), ("add", 3), ("finish", 1), ("finish", 3),
+)
 SPAN = 1152
 MESH = pl.DeviceIdType.MESH
 F32 = jnp.float32
@@ -114,7 +121,9 @@
     def greet(other):
         pl.semaphore_signal(barrier, inc=1, device_id=other, device_id_type=MESH)
 
-    for other in (right, left, across, sibling):
+    straight = any(c[1] for c in GATHER + SCATTER)
+    ring = (right, left, sibling) + ((across,) if straight else ())
+    for other in ring:
         greet(other)
     for other, there in (
         (ahead, has_ahead), (behind, has_behind), (ahead2, has_ahead2), (behind2, has_behind2)
@@ -168,7 +177,7 @@
     kv[:, :, nkv:] = jnp.ones((2, kv.shape[1], HEAD), BF16)
     kv[:, 6 * tok:, 0:nkv] = jnp.zeros((2, kv.shape[1] - 6 * tok, nkv), BF16)
 
-    others = 4
+    others = len(ring)
     for there in (has_ahead, has_behind, has_ahead2, has_behind2):
         others = others + jnp.where(there, 1, 0)
     pl.semaphore_wait(barrier, others)
@@ -316,6 +325,10 @@
         landed(fars[c])
         far_keys(c)
 
+    def settle(early):
+        for kind, late in ((2, 1), (3, 2), (4, 3)):
+            landed(kvs[kind][:count - late] if early else kvs[kind][count - late:])
+
     steps = {
         "send": start_near, "near": wait_near, "sum": near_keys, "far": wait_far,
         "pass": pass_on, "share": pass_far, "query": project_queries,
@@ -325,10 +338,11 @@
     for step, index in order:
         if step in needs:
             loaded(needs.pop(step))
+        if (step, index) == ("pass", count - 1):
+            settle(True)
         steps[step](index)
     loaded("out")
-    for kind in (2, 3, 4):
-        landed(kvs[kind])
+    settle(False)
 
     def attend(c):
         if "att" in OFF:
@@ -398,31 +412,28 @@
             total = total + full_o[at].astype(F32)
         out_v[at] = (own_p[at] + total).astype(BF16)
 
-    for c in range(parts):
-        attend(c)
+    def send_far(c):
         output_part(c, 3, far_s)
         start(far_copies[c])
-        if c >= 1 and not SCATTER[c - 1][1]:
-            add_halves(c - 1)
-        if SCATTER[c][1]:
-            output_part(c, 1, right_s)
-            start(sum_copies[c][:1])
-            output_part(c, 2, left_s)
-            start(sum_copies[c][1:])
-        else:
-            output_part(c, 1, right_p)
-            output_part(c, 2, left_p)
-        if c >= 1:
-            output_part(c - 1, 0, own_p)
-        if c >= 2:
-            finish(c - 2)
-    if not SCATTER[-1][1]:
-        add_halves(parts - 1)
-    output_part(parts - 1, 0, own_p)
-    finish(parts - 2)
-    finish(parts - 1)
+
+    def toward(side):
+        def act(c):
+            straight = SCATTER[c][1]
+            ref = ((right_p, left_p), (right_s, left_s))[straight][side]
+            output_part(c, 1 + side, ref)
+            if straight:
+                start(sum_copies[c][side:side + 1])
+        return act
+
+    steps = {
+        "attend": attend, "far": send_far, "right": toward(0), "left": toward(1),
+        "own": lambda c: output_part(c, 0, own_p), "add": add_halves, "finish": finish,
+    }
+    for step, index in SCATTER_ORDER[:-1]:
+        steps[step](index)
     for move in started:
         move.sent()
+    steps[SCATTER_ORDER[-1][0]](SCATTER_ORDER[-1][1])
 
 
 def body(n_seq, n_tp, hidden_in, doc_lengths, w_query, w_key, w_value, w_out):

time: 60.9 us -> 60.8 us (level)
  no operation moved by 1% of the time
where the time goes in v5:
time: 60.8 us; the launch traced here: 60.7 us
  Pallas kernels  59.8 us (98%)
  local copies, waits for them, and re-layouts  0.8 us (1%)
    pallas_call x1, Pallas kernels, body(): pl.pallas_call(functools.partial(layer, n_seq, n_tp), out_shape=pltpu.VME...  59.8 us

profile of v5, /device:TPU:8, one launch (start us, length us, event | category | flops | bytes accessed | tf_op | source)
XLA Modules:
  0.0 60.7 jit_solution(4653154216536680240)
XLA Ops:
  0.0 59.8 %layer.1 = bf16[256,1024]{1,0:T(8,128)(2,1)S(1)} custom-call(s32[64]{0:T(128)} %len_ref.1, f32[1,128]{1,0:T(1,128)} %constant.2.clone.freq_ref, bf16[256,1024]{1,0:T(8,128)(2,1)} %hid_hbm.1, bf16[4096,1024]{1,0:T(8,128)(2,1)} %wq_hbm.1, bf16[4096,256]{1,0:T(8,128)(2,1)} %wk_hbm.1, bf16[4096,256]{1,0:T(8,128)(2,1)} %wv_hbm.1, bf16[1024,4096]{1,0:T(8,128)(2,1)} %wo_hbm.1), custom_call_target="tpu_custom_call" | custom-call | flops 7000000000 | bytes 22000000 | tf_op jit(solution)/shard_map/layer/pallas_call | solution.py:446
  59.9 0.8 %copy.9 = bf16[256,1024]{1,0:T(8,128)(2,1)} copy(bf16[256,1024]{1,0:T(8,128)(2,1)S(1)} %layer.1) | data formatting | bytes 1048576
